TPU v7x, 32 devices: a whole 2x2x4 slice. The times are simulated.
32 devices in a mesh: slab: 8 (over z, y), rep: 4 (over x, core).
Axes of the slice: x: 2, y: 2, z: 4, core: 2. Of those that a mesh axis runs over, the one named last changes fastest.
Arguments:
- saved_input: bfloat16 [4, 6, 1, 256, 256, 256], P('rep', None, None, 'slab'), may hold values from -6 to 6
- output_grad: bfloat16 [4, 6, 1, 256, 256, 256], P('rep', None, None, 'slab'), may hold values from -6 to 6
- spectral_weight: float32 [1024, 8, 1, 1, 32], P('slab'), may hold values from -18 to 18
- bypass_weight: float32 [8, 1, 1], replicated, may hold values from -1.8 to 1.8
Outputs:
- input_grad: bfloat16 [4, 6, 1, 256, 256, 256], P('rep', None, None, 'slab')
- weight_grad: float32 [1024, 8, 1, 1, 32], P('slab')
All inputs are finite; a program needn't handle non-finite values.
Results may differ from a plain program's by a relative error of at most 0.001.
Values sent between devices are 32-bit elements; how exact they have to be, the bound alone decides.
A program may use at most 320 MiB of HBM per device.

v0:
```python
import math

import jax
import jax.numpy as jnp
from jax import lax
from jax.sharding import PartitionSpec as P

NZ = 256
KM = 32


HIGHEST_PRECISION = lax.Precision.HIGHEST


def frequencies(number):
    counter = lax.iota(jnp.int32, number)
    return jnp.where(counter < number // 2, counter, counter - number)


def phase_table(positions, number, length):
    phases = positions[:, None] * frequencies(number)[None, :] % length
    angles = phases.astype(jnp.float32) * (2.0 * math.pi / length)
    return (jnp.cos(angles), jnp.sin(angles))


def cross_three(left, right):
    return (
        left[1] * right[2] - left[2] * right[1],
        left[2] * right[0] - left[0] * right[2],
        left[0] * right[1] - left[1] * right[0],
    )


def cross_pair(left_real, left_imag, right_real, right_imag):
    first = cross_three(left_real, right_real)
    second = cross_three(left_imag, right_imag)
    third = cross_three(left_real, right_imag)
    fourth = cross_three(left_imag, right_real)
    real_part = tuple((first[axis_id] - second[axis_id] for axis_id in range(3)))
    imag_part = tuple((third[axis_id] + fourth[axis_id] for axis_id in range(3)))
    return (real_part, imag_part)


def adjoint_product(scalar_real, scalar_imag, vector_real, vector_imag, grad_real, grad_imag):
    cross_real, cross_imag = cross_pair(
        vector_real, tuple((-entry for entry in vector_imag)), grad_real, grad_imag
    )
    real_part = tuple(
        (
            scalar_real * grad_real[axis_id]
            + scalar_imag * grad_imag[axis_id]
            - cross_imag[axis_id]
            for axis_id in range(3)
        )
    )
    imag_part = tuple(
        (
            scalar_real * grad_imag[axis_id]
            - scalar_imag * grad_real[axis_id]
            + cross_real[axis_id]
            for axis_id in range(3)
        )
    )
    return (real_part, imag_part)


def plane_modes(fields, factor):
    count_first, count_second = (fields.shape[3], fields.shape[4])
    half_comps = fields.shape[1] // 2
    cosine_second, sine_second = phase_table(lax.iota(jnp.int32, count_second), KM, count_second)
    cosine_first, sine_first = phase_table(lax.iota(jnp.int32, count_first), KM, count_first)
    tables_second = jnp.concatenate([cosine_second, sine_second], axis=1)
    along_second = jnp.einsum("fczxy,yk->fczxk", fields, tables_second, precision=HIGHEST_PRECISION)
    real_part = along_second[:, :half_comps, :, :, :KM] + along_second[:, half_comps:, :, :, KM:]
    imag_part = along_second[:, half_comps:, :, :, :KM] - along_second[:, :half_comps, :, :, KM:]
    stacked = jnp.concatenate([real_part, imag_part], axis=1)
    with_cos = jnp.einsum("fczxk,xm->fczmk", stacked, cosine_first, precision=HIGHEST_PRECISION)
    with_sin = jnp.einsum("fczxk,xm->fczmk", stacked, sine_first, precision=HIGHEST_PRECISION)
    real_part = with_cos[:, :half_comps] + with_sin[:, half_comps:]
    imag_part = with_cos[:, half_comps:] - with_sin[:, :half_comps]
    modes = jnp.concatenate([real_part, imag_part], axis=1) * factor
    return modes.reshape(modes.shape[0], fields.shape[1], modes.shape[2], KM * KM)


def depth_forward(block, cosine_depth, sine_depth):
    half_comps = block.shape[1] // 2
    with_cos = jnp.einsum("fczr,zk->rfck", block, cosine_depth, precision=HIGHEST_PRECISION)
    with_sin = jnp.einsum("fczr,zk->rfck", block, sine_depth, precision=HIGHEST_PRECISION)
    real_part = with_cos[:, :, :half_comps] + with_sin[:, :, half_comps:]
    imag_part = with_cos[:, :, half_comps:] - with_sin[:, :, :half_comps]
    return jnp.concatenate([real_part, imag_part], axis=2)


def depth_inverse(rows_block, cosine_depth, sine_depth):
    half_comps = rows_block.shape[1] // 2
    with_cos = jnp.einsum("rck,zk->czr", rows_block, cosine_depth, precision=HIGHEST_PRECISION)
    with_sin = jnp.einsum("rck,zk->czr", rows_block, sine_depth, precision=HIGHEST_PRECISION)
    real_part = with_cos[:half_comps] - with_sin[half_comps:]
    imag_part = with_cos[half_comps:] + with_sin[:half_comps]
    return jnp.concatenate([real_part, imag_part], axis=0)


def shards(saved_input, output_grad, spectral_weight, bypass_weight):
    channels = saved_input.shape[2]
    planes, count_first, count_second = (
        saved_input.shape[3],
        saved_input.shape[4],
        saved_input.shape[5],
    )
    components = 6 * channels
    half_comps = 3 * channels
    factor = 1.0 / math.sqrt(count_first * count_second * NZ)
    rows_owned = spectral_weight.shape[0]
    fields = jnp.concatenate([saved_input, output_grad], axis=0).astype(jnp.float32)
    fields = fields.reshape(2, components, planes, count_first, count_second)
    modes = plane_modes(fields, factor)
    slab_start = lax.axis_index("slab") * planes
    cosine_depth, sine_depth = phase_table(slab_start + lax.iota(jnp.int32, planes), KM, NZ)
    spectra = lax.psum_scatter(
        depth_forward(modes, cosine_depth, sine_depth), "slab", scatter_dimension=0, tiled=True
    )
    parts = spectra.reshape(rows_owned, 2, 2, 3, channels, KM)
    inputs_real = tuple((parts[:, 0, 0, axis_id][:, None] for axis_id in range(3)))
    inputs_imag = tuple((parts[:, 0, 1, axis_id][:, None] for axis_id in range(3)))
    grads_real = tuple((parts[:, 1, 0, axis_id][:, :, None] for axis_id in range(3)))
    grads_imag = tuple((parts[:, 1, 1, axis_id][:, :, None] for axis_id in range(3)))
    scalar_real = sum(
        (
            inputs_real[axis_id] * grads_real[axis_id] + inputs_imag[axis_id] * grads_imag[axis_id]
            for axis_id in range(3)
        )
    )
    scalar_imag = sum(
        (
            inputs_real[axis_id] * grads_imag[axis_id] - inputs_imag[axis_id] * grads_real[axis_id]
            for axis_id in range(3)
        )
    )
    cross_real, cross_imag = cross_pair(
        inputs_real, tuple((-entry for entry in inputs_imag)), grads_real, grads_imag
    )
    local_grad = jnp.stack(
        [scalar_real] + list(cross_imag) + [scalar_imag] + [-entry for entry in cross_real], axis=1
    )
    weight_grad = lax.psum(local_grad, "rep")
    weight_vector_real = tuple((spectral_weight[:, 1 + axis_id] for axis_id in range(3)))
    weight_vector_imag = tuple((spectral_weight[:, 5 + axis_id] for axis_id in range(3)))
    mode_real, mode_imag = adjoint_product(
        spectral_weight[:, 0],
        spectral_weight[:, 4],
        weight_vector_real,
        weight_vector_imag,
        grads_real,
        grads_imag,
    )
    mode_grads = jnp.stack(
        [jnp.sum(entry, axis=1) for entry in list(mode_real) + list(mode_imag)], axis=1
    )
    mode_grads = mode_grads.reshape(rows_owned, components, KM)
    depth_modes = depth_inverse(
        lax.all_gather(mode_grads, "slab", axis=0, tiled=True), cosine_depth, sine_depth
    )
    cosine_second, sine_second = phase_table(lax.iota(jnp.int32, count_second), KM, count_second)
    cosine_first, sine_first = phase_table(lax.iota(jnp.int32, count_first), KM, count_first)
    grid_modes = depth_modes.reshape(components, planes, KM, KM)
    with_cos = jnp.einsum("czmk,xm->czxk", grid_modes, cosine_first, precision=HIGHEST_PRECISION)
    with_sin = jnp.einsum("czmk,xm->czxk", grid_modes, sine_first, precision=HIGHEST_PRECISION)
    stacked = jnp.concatenate(
        [
            with_cos[:half_comps] - with_sin[half_comps:],
            with_cos[half_comps:] + with_sin[:half_comps],
        ],
        axis=0,
    )
    with_cos = jnp.einsum("czxk,yk->czxy", stacked, cosine_second, precision=HIGHEST_PRECISION)
    with_sin = jnp.einsum("czxk,yk->czxy", stacked, sine_second, precision=HIGHEST_PRECISION)
    spectral_real = (with_cos[:half_comps] - with_sin[half_comps:]) * factor
    spectral_imag = (with_cos[half_comps:] + with_sin[:half_comps]) * factor
    cotangent = fields[1].reshape(2, 3, channels, planes, count_first, count_second)
    field_real = tuple((cotangent[0, axis_id][:, None] for axis_id in range(3)))
    field_imag = tuple((cotangent[1, axis_id][:, None] for axis_id in range(3)))

    def expand(entry):
        return entry[:, :, None, None, None]

    bypass_vector_real = tuple((expand(bypass_weight[1 + axis_id]) for axis_id in range(3)))
    bypass_vector_imag = tuple((expand(bypass_weight[5 + axis_id]) for axis_id in range(3)))
    bypass_real, bypass_imag = adjoint_product(
        expand(bypass_weight[0]),
        expand(bypass_weight[4]),
        bypass_vector_real,
        bypass_vector_imag,
        field_real,
        field_imag,
    )
    bypass_real = jnp.stack([jnp.sum(entry, axis=0) for entry in bypass_real], axis=0).reshape(
        half_comps, planes, count_first, count_second
    )
    bypass_imag = jnp.stack([jnp.sum(entry, axis=0) for entry in bypass_imag], axis=0).reshape(
        half_comps, planes, count_first, count_second
    )
    total_real = spectral_real + bypass_real
    total_imag = spectral_imag + bypass_imag
    input_grad = jnp.concatenate([total_real, total_imag], axis=0).astype(jnp.bfloat16)
    input_grad = input_grad.reshape(1, 6, channels, planes, count_first, count_second)
    return (input_grad, weight_grad)


def solution(mesh):
    placed = (
        P("rep", None, None, "slab", None, None),
        P("rep", None, None, "slab", None, None),
        P("slab", None, None, None, None),
        P(),
    )
    return jax.shard_map(
        shards,
        mesh=mesh,
        in_specs=placed,
        out_specs=(P("rep", None, None, "slab", None, None), P("slab", None, None, None, None)),
        check_vma=False,
    )
```

profile of v0, /device:TPU:0, one launch (start us, length us, event | category | flops | bytes accessed | tf_op | source)
XLA Modules:
  0.0 493.2 jit_solution(4458828581433509608)
XLA Ops:
  7.4 51.5 %fusion = f32[2,6,32,256,64]{3,4,2,1,0:T(8,128)} fusion(bf16[1,6,1,32,256,256]{5,4,3,1,0,2:T(8,128)(2,1)} %bitcast.615, bf16[1,6,1,32,256,256]{5,4,3,1,0,2:T(8,128)(2,1)} %bitcast.631, f32[256,32]{0,1:T(8,128)S(1)} %get-tuple-element.23, f32[256,32]{0,1:T(8,128)S(1)} %get-tuple-element.22), kind=kOutput, calls=%fused_computation.1 | convolution fusion | flops 19352535040 | bytes 75563008 | tf_op jit(solution)/shard_map/fczxy,yk->fczxk/dot_general | solution.py:73
  59.0 10.1 %slice_add_fusion.1 = (f32[2,3,32,256,32]{3,4,2,1,0:T(8,128)S(1)}, f32[2,3,32,256,32]{3,4,2,1,0:T(8,128)S(1)}) fusion(f32[2,6,32,256,64]{3,4,2,1,0:T(8,128)} %fusion), kind=kLoop, calls=%fused_computation.27 | loop fusion | flops 3145728 | bytes 37748736 | tf_op jit(solution)/shard_map/add | solution.py:74
  69.0 29.5 %fusion.16 = f32[2,6,32,32,32]{4,3,2,1,0:T(8,128)S(1)} fusion(f32[2,3,32,256,32]{3,4,2,1,0:T(8,128)S(1)} %get-tuple-element.13, f32[2,3,32,256,32]{3,4,2,1,0:T(8,128)S(1)} %get-tuple-element.12, s32[32]{0:T(128)S(1)} %get-tuple-element.32), kind=kOutput, calls=%fused_computation.36 | convolution fusion | flops 1211219968 | bytes 14155904 | tf_op jit(solution)/shard_map/fczxk,xm->fczmk/dot_general | solution.py:78
  98.5 30.8 %fusion.15 = f32[2,6,32,32,32]{4,3,2,1,0:T(8,128)} fusion(f32[2,3,32,256,32]{3,4,2,1,0:T(8,128)S(1)} %get-tuple-element.13, f32[2,3,32,256,32]{3,4,2,1,0:T(8,128)S(1)} %get-tuple-element.12, s32[32]{0:T(128)S(1)} %get-tuple-element.32), kind=kOutput, calls=%fused_computation.35 | convolution fusion | flops 1211219968 | bytes 14155904 | tf_op jit(solution)/shard_map/fczxk,xm->fczmk/dot_general | solution.py:77
  129.3 7.1 %slice_add_fusion.3 = (f32[2,3,32,32,32]{4,3,2,1,0:T(8,128)}, f32[2,3,32,32,32]{4,3,2,1,0:T(8,128)}) fusion(f32[2,6,32,32,32]{4,3,2,1,0:T(8,128)S(1)} %fusion.16, f32[2,6,32,32,32]{4,3,2,1,0:T(8,128)} %fusion.15), kind=kLoop, calls=%fused_computation.34 | loop fusion | flops 393216 | bytes 4718592 | tf_op jit(solution)/shard_map/add | solution.py:79
  136.4 3.3 concatenate.52
  139.7 2.9 concatenate.53
  142.6 1.6 convolution_bitcast_fusion.2
  144.2 1.6 convolution_bitcast_fusion.3
  146.1 1.2 pad_maximum_fusion.10
  150.1 27.0 %convert.12 = f32[2,3,1,32,256,256]{5,4,3,2,1,0:T(8,128)} convert(bf16[2,3,1,32,256,256]{5,4,3,2,1,0:T(8,128)(2,1)} %bitcast.616) | non-fusion elementwise | flops 12582912 | bytes 75497472 | tf_op jit(solution)/shard_map/reshape;squeeze | solution.py:179
  177.1 26.4 %subtract_bitcast_fusion.2 = (f32[1,1,32,256,256]{4,3,2,0,1:T(8,128)}, f32[1,1,32,256,256]{4,3,2,1,0:T(8,128)}) fusion(f32[2,3,1,32,256,256]{5,4,3,2,1,0:T(8,128)} %convert.12, f32[]{:T(128)} %bitcast.55, f32[]{:T(128)} %bitcast.54, f32[]{:T(128)} %bitcast.53, f32[]{:T(128)} %bitcast.52, f32[]{:T(128)} %bitcast.50, f32[]{:T(128)} %bitcast.48), kind=kLoop, calls=%fused_computation.25 | loop fusion | flops 46137344 | bytes 67108888 | tf_op jit(solution)/shard_map/sub | solution.py:50
  203.5 26.2 %subtract_bitcast_fusion.1 = (f32[1,1,32,256,256]{4,3,2,0,1:T(8,128)}, f32[1,1,32,256,256]{4,3,2,1,0:T(8,128)}) fusion(f32[2,3,1,32,256,256]{5,4,3,2,1,0:T(8,128)} %convert.12, f32[]{:T(128)} %bitcast.59, f32[]{:T(128)} %bitcast.58, f32[]{:T(128)} %bitcast.55, f32[]{:T(128)} %bitcast.53, f32[]{:T(128)} %bitcast.50, f32[]{:T(128)} %bitcast.48), kind=kLoop, calls=%fused_computation.24 | loop fusion | flops 46137344 | bytes 67108888 | tf_op jit(solution)/shard_map/sub | solution.py:50
  229.8 26.2 %subtract_bitcast_fusion = (f32[1,1,32,256,256]{4,3,2,0,1:T(8,128)}, f32[1,1,32,256,256]{4,3,2,1,0:T(8,128)}) fusion(f32[2,3,1,32,256,256]{5,4,3,2,1,0:T(8,128)} %convert.12, f32[]{:T(128)} %bitcast.59, f32[]{:T(128)} %bitcast.58, f32[]{:T(128)} %bitcast.54, f32[]{:T(128)} %bitcast.52, f32[]{:T(128)} %bitcast.50, f32[]{:T(128)} %bitcast.48), kind=kLoop, calls=%fused_computation.23 | loop fusion | flops 46137344 | bytes 67108888 | tf_op jit(solution)/shard_map/sub | solution.py:50
  261.8 33.9 %all-gather = f32[1024,6,1,32]{0,3,1,2:T(8,128)S(1)} all-gather(f32[128,6,1,32]{0,3,1,2:T(8,128)S(1)} %constant_dynamic-update-slice_fusion), channel_id=2, replica_groups=mesh['slab'=8,'rep'=4] {'slab'}, dimensions={0}, use_global_device_ids=true | all-gather | bytes 884736 | tf_op jit(solution)/shard_map/all_gather | solution.py:161
  298.7 2.1 reshape.2626
  300.8 5.5 %convolution_bitcast_fusion = f32[6,32,256,32]{2,3,1,0:T(8,128)S(1)} fusion(f32[6,32,32,32]{3,2,1,0:T(8,128)S(1)} %reshape.2626, s32[32]{0:T(128)S(1)} %get-tuple-element.32), kind=kOutput, calls=%fused_computation.37 | convolution fusion | flops 604094464 | bytes 7078016 | tf_op jit(solution)/shard_map/czmk,xm->czxk/dot_general | solution.py:167
  306.3 7.3 %convolution_bitcast_fusion.1 = f32[6,32,256,32]{2,3,1,0:T(8,128)} fusion(f32[6,32,32,32]{3,2,1,0:T(8,128)S(1)} %reshape.2626, s32[32]{0:T(128)S(1)} %get-tuple-element.32), kind=kOutput, calls=%fused_computation.38 | convolution fusion | flops 604094464 | bytes 7078016 | tf_op jit(solution)/shard_map/czmk,xm->czxk/dot_general | solution.py:166
  313.6 4.4 slice_subtract_fusion.2
  318.0 44.6 %fusion.13 = f32[6,32,256,256]{3,2,1,0:T(8,128)} fusion(f32[3,32,256,32]{2,3,1,0:T(8,128)S(1)} %get-tuple-element.15, f32[3,32,256,32]{2,3,1,0:T(8,128)S(1)} %get-tuple-element.14, s32[32]{0:T(128)S(1)} %get-tuple-element.32), kind=kOutput, calls=%fused_computation.29 | convolution fusion | flops 4833525760 | bytes 56623232 | tf_op jit(solution)/shard_map/czxk,yk->czxy/dot_general | solution.py:176
  362.6 44.7 %fusion.14 = f32[6,32,256,256]{3,2,1,0:T(8,128)} fusion(f32[3,32,256,32]{2,3,1,0:T(8,128)S(1)} %get-tuple-element.15, f32[3,32,256,32]{2,3,1,0:T(8,128)S(1)} %get-tuple-element.14, s32[32]{0:T(128)S(1)} %get-tuple-element.32), kind=kOutput, calls=%fused_computation.30 | convolution fusion | flops 4833525760 | bytes 56623232 | tf_op jit(solution)/shard_map/czxk,yk->czxy/dot_general | solution.py:175
  408.1 55.7 %fusion.9 = (bf16[1,3,1,32,256,256]{5,4,3,1,2,0:T(8,128)(2,1)}, bf16[1,3,1,32,256,256]{5,4,3,1,2,0:T(8,128)(2,1)}) fusion(f32[1,1,32,256,256]{4,3,2,0,1:T(8,128)} %get-tuple-element.10, f32[1,1,32,256,256]{4,3,2,0,1:T(8,128)} %get-tuple-element.8, f32[1,1,32,256,256]{4,3,2,0,1:T(8,128)} %get-tuple-element.6, f32[6,32,256,256]{3,2,1,0:T(8,128)} %fusion.13, ...), kind=kLoop, calls=%fused_computation.16 | loop fusion | flops 75497472 | bytes 176160768 | tf_op jit(solution)/shard_map/concatenate | solution.py:204
  463.8 20.5 %maximum_bitcast_fusion.4 = bf16[1,6,1,32,256,256]{5,4,3,2,1,0:T(8,128)(2,1)} fusion(bf16[1,3,1,32,256,256]{5,4,3,1,2,0:T(8,128)(2,1)} %get-tuple-element.5, bf16[1,3,1,32,256,256]{5,4,3,1,2,0:T(8,128)(2,1)} %get-tuple-element.4), kind=kLoop, calls=%fused_computation.14 | loop fusion | flops 12582912 | bytes 50331648
  484.3 1.6 copy.51
  (36 shorter events, 10.9 us)
Async XLA Ops:
  7.2 248.8 %reduce-scatter.2.cloned.1.call-start = ((), (), s32[]{:S(2)}) async-start(), calls=%async_computation.1 | async-start | bytes 1769472 | tf_op jit(solution)/shard_map/reduce_scatter | solution.py:119
  142.6 4.9 copy-start.3
  147.4 336.9 %all-reduce.2.cloned.1.call-start = ((), (), s32[]{:S(2)}) async-start(), calls=%async_computation.2 | async-start | bytes 262144 | tf_op jit(solution)/shard_map/psum | solution.py:145
  229.8 27.1 %copy-start.1 = (f32[128,8,1,1,32]{0,4,3,2,1:T(8,128)S(1)}, f32[128,8,1,1,32]{0,4,3,2,1:T(8,128)}, u32[]{:S(2)}) copy-start(f32[128,8,1,1,32]{0,4,3,2,1:T(8,128)} %param.6) | copy-start | bytes 393220
  362.6 44.7 %copy-start = (f32[128,2,6,32]{0,3,2,1:T(8,128)S(1)}, f32[128,2,6,32]{0,3,2,1:T(8,128)}, u32[]{:S(2)}) copy-start(f32[128,2,6,32]{0,3,2,1:T(8,128)} %reduce-scatter.2.cloned.1.call-done) | copy-start | bytes 589828
  407.4 0.7 copy-start.2
Sparse Core Ops, SparseCore 0:
  147.5 68.2 reduce-scatter.1
  408.2 32.4 all-reduce.1
where the time goes:
time: 500 us; the launch traced here: 493 us
  matrix products  219 us (44%)
  other arithmetic  212 us (42%)
  blocking collectives  33.9 us (7%)
  between operations  16.7 us (3%)
  local copies, waits for them, and re-layouts  11.2 us (2%)
    sub x3, other arithmetic, adjoint_product(): scalar_real * grad_real[axis_id] + scalar_imag * grad_imag[axis_id]  78.8 us
    concatenate x1, other arithmetic, shards(): jnp.concatenate([total_real, total_imag], axis=0).astype(jnp.bfloat16)  55.7 us
    dot_general x1, matrix products, plane_modes(): jnp.einsum('fczxy,yk->fczxk', fields, tables_second, precision=HIGHEST_PR...  51.5 us
    dot_general x1, matrix products, shards(): jnp.einsum('czxk,yk->czxy', stacked, cosine_second, precision=HIGHEST_PRE...  44.7 us
    dot_general x1, matrix products, shards(): jnp.einsum('czxk,yk->czxy', stacked, sine_second, precision=HIGHEST_PRECI...  44.6 us
    all_gather x1, blocking collectives, shards(): lax.all_gather(mode_grads, 'slab', axis=0, tiled=True)  33.9 us
    dot_general x1, matrix products, plane_modes(): jnp.einsum('fczxk,xm->fczmk', stacked, cosine_first, precision=HIGHEST_PR...  30.8 us
    dot_general x1, matrix products, plane_modes(): jnp.einsum('fczxk,xm->fczmk', stacked, sine_first, precision=HIGHEST_PREC...  29.5 us
  transfers between devices with their start and end apart: 2, of which 0 were waited for; matrix products, arithmetic and copies ran while one was open for 37% of the time, Pallas kernels for 0%

commit v1 on v0

v1 whole, which is shorter than its diff:
```python
import functools
import math

import jax
import jax.numpy as jnp
import numpy as np
from jax import lax
from jax.experimental import pallas as pl
from jax.experimental.pallas import tpu as pltpu
from jax.sharding import PartitionSpec as P

NZ = 256
KM = 32
F32 = jnp.float32
BF16 = jnp.bfloat16


def table(length):
    counter = np.arange(KM)
    freqs = np.where(counter < KM // 2, counter, counter - KM)
    angles = (np.arange(length)[:, None] * freqs[None, :] % length) * (2.0 * math.pi / length)
    return np.cos(angles), np.sin(angles)


def halves(values):
    values = np.asarray(values, np.float32)
    high = values.astype(BF16)
    return high, (values - high.astype(np.float32)).astype(BF16)


def split(values):
    high = values.astype(BF16)
    return high, (values - high.astype(F32)).astype(BF16)


def dot(left, right):
    return jnp.dot(left, right, preferred_element_type=F32)


def turn(values, sign):
    half = values.shape[-1] // 2
    return jnp.concatenate([-sign * values[..., half:], sign * values[..., :half]], axis=-1)


class Plan:
    def __init__(self, nx, ny, planes, rows_owned):
        self.nx, self.ny, self.planes = nx, ny, planes
        self.zb = min(8, planes)
        self.shares = max(1, KM // rows_owned)
        per_owner = max(1, rows_owned // KM)
        self.lane_groups = min(2, per_owner)
        self.owned_pairs = per_owner // self.lane_groups
        self.owners = KM // per_owner
        self.pairs = KM // self.lane_groups
        self.lanes = 2 * self.lane_groups * KM
        groups = self.lane_groups
        factor = 1.0 / math.sqrt(nx * ny * NZ)
        cos_x, sin_x = table(nx)
        cos_y, sin_y = table(ny)
        order = np.concatenate([np.arange(g, KM, groups) for g in range(groups)])
        cos_x, sin_x = cos_x[:, order], sin_x[:, order]
        from_real = np.concatenate([cos_x.T, -sin_x.T], 0) * factor
        from_imag = np.concatenate([sin_x.T, cos_x.T], 0) * factor
        self.fwd_x = np.stack(
            [np.concatenate(halves(from_real), 0), np.concatenate(halves(from_imag), 0)], 0
        )
        fwd_y = np.zeros((2, groups, ny, 2, groups, KM))
        inv_y = np.zeros((2, groups, KM, 2, groups, ny))
        for g in range(groups):
            fwd_y[0, g, :, 0, g] = cos_y
            fwd_y[0, g, :, 1, g] = -sin_y
            fwd_y[1, g, :, 0, g] = sin_y
            fwd_y[1, g, :, 1, g] = cos_y
            inv_y[0, g, :, 0, g] = cos_y.T
            inv_y[0, g, :, 1, g] = sin_y.T
            inv_y[1, g, :, 0, g] = -sin_y.T
            inv_y[1, g, :, 1, g] = cos_y.T
        fwd_y = fwd_y.reshape(2 * groups, ny, self.lanes)
        self.fwd_y = np.concatenate(halves(fwd_y), -1)
        inv_y = inv_y.reshape(self.lanes, 2 * groups * ny)
        inv_high, inv_low = halves(inv_y)
        self.inv_y = np.concatenate([inv_high, inv_high, inv_low], 0)
        inv_x = np.concatenate(
            [np.concatenate([cos_x, -sin_x], 1), np.concatenate([sin_x, cos_x], 1)], 0
        ) * factor
        high, low = halves(inv_x)
        self.inv_x = np.concatenate([high, high, low], 1)
        cos_z, sin_z = table(NZ)
        self.fwd_z = np.stack(halves(np.concatenate([cos_z, sin_z], 1)), 0)


def forward_kernel(plan, field, tab_x, tab_y, tab_z, out, along_x, along_xy):
    group = pl.program_id(1)
    rows = 2 * KM
    pairs, lanes, zb = plan.pairs, plan.lanes, plan.zb
    for z in range(zb):
        both = dot(tab_x[0], field[0, 0, z]) + dot(tab_x[1], field[1, 0, z])
        summed = both[:rows] + both[rows:]
        for part in range(plan.ny // 128):
            along_x[part, pl.ds(z, rows, stride=zb), :] = summed[:, part * 128 : part * 128 + 128]
    block = pairs * zb
    wide, narrow = 0.0, 0.0
    for g in range(rows // pairs):
        values = jnp.concatenate(
            [along_x[part, g * block : (g + 1) * block] for part in range(plan.ny // 128)], axis=1
        )
        high, low = split(values)
        wide = wide + dot(high, tab_y[g])
        narrow = narrow + dot(low, tab_y[g, :, :lanes])
    modes = wide[:, :lanes] + wide[:, lanes:] + narrow
    along_xy[:, pl.ds(pl.multiple_of(group * zb, zb), zb), :] = modes.reshape(pairs, zb, lanes)

    @pl.when(group == plan.planes // plan.zb - 1)
    def _():
        for pair in range(pairs):
            high, low = split(along_xy[pair])
            turned = dot(tab_z[0], high) + dot(tab_z[1], high) + dot(tab_z[0], low)
            out[pair // plan.owned_pairs, 0, pair % plan.owned_pairs] = turned[:KM] + turn(
                turned[KM:], -1.0
            )


def forward_modes(plan, field, tab_z):
    planes, nx, ny = plan.planes, plan.nx, plan.ny
    whole = lambda k, g: (0, 0, 0)
    return pl.pallas_call(
        functools.partial(forward_kernel, plan),
        grid=(3, planes // plan.zb),
        in_specs=[
            pl.BlockSpec((2, 1, plan.zb, nx, ny), lambda k, g: (0, k, g, 0, 0)),
            pl.BlockSpec(plan.fwd_x.shape, whole),
            pl.BlockSpec(plan.fwd_y.shape, whole),
            pl.BlockSpec((2, 2 * KM, planes), whole),
        ],
        out_specs=pl.BlockSpec(
            (plan.owners, 1, plan.owned_pairs, KM, plan.lanes), lambda k, g: (0, k, 0, 0, 0)
        ),
        out_shape=jax.ShapeDtypeStruct(
            (plan.owners, 3, plan.owned_pairs, KM, plan.lanes), F32
        ),
        scratch_shapes=[
            pltpu.VMEM((ny // 128, 2 * KM * plan.zb, 128), F32),
            pltpu.VMEM((plan.pairs, planes, plan.lanes), F32),
        ],
        compiler_params=pltpu.CompilerParams(vmem_limit_bytes=40 * 2**20),
        cost_estimate=pl.CostEstimate(
            flops=2 * 6 * planes * nx * ny * 128, bytes_accessed=12 * planes * nx * ny,
            transcendentals=0,
        ),
    )(field, jnp.asarray(plan.fwd_x), jnp.asarray(plan.fwd_y), tab_z)


def bypass_terms(weight, real, imag):
    s_r, s_i = weight[0], weight[4]
    v_r = [weight[1 + axis] for axis in range(3)]
    v_i = [weight[5 + axis] for axis in range(3)]
    outs_r, outs_i = [], []
    for k in range(3):
        a, b = (k + 1) % 3, (k + 2) % 3
        cross_r = (
            v_r[a] * real[b] - v_r[b] * real[a] + v_i[a] * imag[b] - v_i[b] * imag[a]
        )
        cross_i = (
            v_r[a] * imag[b] - v_r[b] * imag[a] - v_i[a] * real[b] + v_i[b] * real[a]
        )
        outs_r.append(s_r * real[k] + s_i * imag[k] - cross_i)
        outs_i.append(s_r * imag[k] - s_i * real[k] + cross_r)
    return outs_r, outs_i


def inverse_kernel(
    plan, step_planes, weight, field, modes, tab_z, tab_y, tab_x, out, along_z, along_zy, spectral
):
    step = pl.program_id(0)
    pairs, lanes, nx, ny, zb = plan.pairs, plan.lanes, plan.nx, plan.ny, plan.zb
    steps = zb // step_planes
    block = pairs * zb

    @pl.when(step == 0)
    def _():
        for pair in range(pairs):
            for k in range(3):
                values = modes[pair // plan.owned_pairs, k, pair % plan.owned_pairs]
                high, low = split(jnp.concatenate([values, turn(values, 1.0)], axis=0))
                along_z[k, pair] = dot(tab_z[0], high) + dot(tab_z[1], high) + dot(tab_z[0], low)

    @pl.when(step % steps == 0)
    def _():
        start = pl.multiple_of(step * step_planes, zb)
        for k in range(3):
            values = along_z[k, :, pl.ds(start, zb), :].reshape(block, lanes)
            high, low = split(values)
            parts = jnp.concatenate([high, low, high], axis=1)
            for g in range(2 * plan.lane_groups):
                result = dot(parts, tab_y[:, g * ny : (g + 1) * ny])
                for part in range(ny // 128):
                    along_zy[k, part, g * block : (g + 1) * block] = result[
                        :, part * 128 : part * 128 + 128
                    ]

    for z in range(step_planes):
        where = (step % steps) * step_planes + z
        for k in range(3):
            values = jnp.concatenate(
                [
                    along_zy[k, part, pl.ds(where, 2 * KM, stride=zb), :]
                    for part in range(ny // 128)
                ],
                axis=1,
            )
            high, low = split(values)
            spectral[z, k] = dot(tab_x[...], jnp.concatenate([high, low, high], axis=0))
        for row in range(0, nx, 16):
            for lane in range(0, ny, 128):
                rows, columns = pl.ds(row, 16), pl.ds(lane, 128)
                real = [field[k, z, rows, columns].astype(F32) for k in range(3)]
                imag = [field[3 + k, z, rows, columns].astype(F32) for k in range(3)]
                outs_r, outs_i = bypass_terms(weight, real, imag)
                for k in range(3):
                    out[k, z, rows, columns] = (outs_r[k] + spectral[z, k, rows, columns]).astype(
                        BF16
                    )
                    out[3 + k, z, rows, columns] = (
                        outs_i[k] + spectral[z, k, pl.ds(nx + row, 16), columns]
                    ).astype(BF16)


def inverse_field(plan, weight, field, modes, tab_z):
    planes, nx, ny = plan.planes, plan.nx, plan.ny
    step_planes = 2
    whole = lambda i: (0, 0)
    return pl.pallas_call(
        functools.partial(inverse_kernel, plan, step_planes),
        grid=(planes // step_planes,),
        in_specs=[
            pl.BlockSpec(memory_space=pltpu.SMEM),
            pl.BlockSpec((6, step_planes, nx, ny), lambda i: (0, i, 0, 0)),
            pl.BlockSpec(modes.shape, lambda i: (0, 0, 0, 0, 0)),
            pl.BlockSpec((2, planes, 2 * KM), lambda i: (0, 0, 0)),
            pl.BlockSpec(plan.inv_y.shape, whole),
            pl.BlockSpec(plan.inv_x.shape, whole),
        ],
        out_specs=pl.BlockSpec((6, step_planes, nx, ny), lambda i: (0, i, 0, 0)),
        out_shape=jax.ShapeDtypeStruct((6, planes, nx, ny), BF16),
        scratch_shapes=[
            pltpu.VMEM((3, plan.pairs, planes, plan.lanes), F32),
            pltpu.VMEM((3, ny // 128, 2 * KM * plan.zb, 128), F32),
            pltpu.VMEM((step_planes, 3, 2 * nx, ny), F32),
        ],
        compiler_params=pltpu.CompilerParams(vmem_limit_bytes=40 * 2**20),
        cost_estimate=pl.CostEstimate(
            flops=2 * 6 * planes * nx * ny * 192, bytes_accessed=24 * planes * nx * ny,
            transcendentals=0,
        ),
    )(weight, field, modes, tab_z, jnp.asarray(plan.inv_y), jnp.asarray(plan.inv_x))


def shards(saved_input, output_grad, spectral_weight, bypass_weight):
    planes, nx, ny = saved_input.shape[3:]
    rows_owned = spectral_weight.shape[0]
    plan = Plan(nx, ny, planes, rows_owned)
    shares = plan.shares
    start = lax.axis_index("slab") * planes
    depth = lax.dynamic_slice_in_dim(jnp.asarray(plan.fwd_z), start, planes, axis=1)
    tab_fwd = jnp.swapaxes(depth, 1, 2)

    def spectrum(field):
        parts = forward_modes(plan, field.reshape(2, 3, planes, nx, ny), tab_fwd)
        if shares > 1:
            parts = parts.reshape(plan.owners, 3, 1, KM, 2, shares, KM // shares)
            parts = jnp.transpose(parts, (0, 5, 1, 2, 3, 4, 6))
            parts = parts.reshape(plan.owners * shares, 3, 1, KM, plan.lanes // shares)
        return lax.psum_scatter(parts, "slab", scatter_dimension=0, tiled=True)[0]

    grads = spectrum(output_grad)
    half = plan.lanes // (2 * shares)
    weights = spectral_weight.reshape(plan.owned_pairs, half, 8, KM)
    weights = jnp.transpose(weights, (2, 0, 3, 1))
    grads_r = [grads[k, :, :, :half] for k in range(3)]
    grads_i = [grads[k, :, :, half:] for k in range(3)]
    mode_r, mode_i = bypass_terms(weights, grads_r, grads_i)
    mode_grads = jnp.stack([jnp.concatenate([r, i], -1) for r, i in zip(mode_r, mode_i)], 0)
    modes = lax.all_gather(mode_grads, "slab", axis=0)
    if shares > 1:
        modes = modes.reshape(plan.owners, shares, 3, 1, KM, 2, KM // shares)
        modes = jnp.transpose(modes, (0, 2, 3, 4, 5, 1, 6))
        modes = modes.reshape(plan.owners, 3, 1, KM, plan.lanes)
    inputs = spectrum(saved_input)
    inputs_r = [inputs[k, :, :, :half] for k in range(3)]
    inputs_i = [inputs[k, :, :, half:] for k in range(3)]
    scalar_r = sum(inputs_r[k] * grads_r[k] + inputs_i[k] * grads_i[k] for k in range(3))
    scalar_i = sum(inputs_r[k] * grads_i[k] - inputs_i[k] * grads_r[k] for k in range(3))
    vector_r, vector_i = [], []
    for k in range(3):
        a, b = (k + 1) % 3, (k + 2) % 3
        vector_r.append(
            inputs_r[a] * grads_i[b] - inputs_r[b] * grads_i[a]
            - inputs_i[a] * grads_r[b] + inputs_i[b] * grads_r[a]
        )
        vector_i.append(
            inputs_r[b] * grads_r[a] - inputs_r[a] * grads_r[b]
            + inputs_i[b] * grads_i[a] - inputs_i[a] * grads_i[b]
        )
    local = jnp.stack([scalar_r] + vector_r + [scalar_i] + vector_i, axis=0)
    local = jnp.transpose(local, (1, 3, 0, 2)).reshape(rows_owned, 8, 1, 1, KM)
    weight_grad = lax.psum(local, "rep")
    input_grad = inverse_field(
        plan, bypass_weight.reshape(8), output_grad.reshape(6, planes, nx, ny), modes, depth
    )
    return (input_grad.reshape(1, 6, 1, planes, nx, ny), weight_grad)


def solution(mesh):
    placed = (
        P("rep", None, None, "slab", None, None),
        P("rep", None, None, "slab", None, None),
        P("slab", None, None, None, None),
        P(),
    )
    return jax.shard_map(
        shards,
        mesh=mesh,
        in_specs=placed,
        out_specs=(P("rep", None, None, "slab", None, None), P("slab", None, None, None, None)),
        check_vma=False,
    )
```

time: 500 us -> 244 us (0.49); the launches traced: 493 us -> 242 us
  matrix products: 219 us -> 0 us
  other arithmetic: 212 us -> 14 us
  waiting for transfers between devices: 0.04 us -> 107 us
  Pallas kernels: 0 us -> 69.5 us
  local copies, waits for them, and re-layouts: 11.2 us -> 5.72 us
    dot_general x11 -> x0, matrix products: 219 us -> none  [the longest x1 51.5 us: plane_modes(): jnp.einsum('fczxy,yk->fczxk', fields, tables_second, precision=HIGHEST_PR...]
    reduce_scatter x1 -> x2, waiting for transfers between devices: 0.01 us -> 107 us  [spectrum(): return lax.psum_scatter(parts, 'slab', scatter_dimension=0, tiled=True)[0]]
    sub x5 -> x3, other arithmetic: 83.3 us -> 2.87 us  [bypass_terms(): outs_r.append(s_r * real[k] + s_i * imag[k] - cross_i)]
    pallas_call x0 -> x3, Pallas kernels: none -> 69.5 us  [the longest x2 34.9 us: forward_modes(): pl.pallas_call(functools.partial(forward_kernel, plan), grid=(3, planes /...]
    concatenate x3 -> x0, other arithmetic: 57.9 us -> none  [the longest x1 55.7 us: shards(): jnp.concatenate([total_real, total_imag], axis=0).astype(jnp.bfloat16)]
    another operation x3 -> x4, other arithmetic: 27.8 us -> 1.15 us  [the longest x1 0.98 us: shards(): local = jnp.stack([scalar_r] + vector_r + [scalar_i] + vector_i, axis=0)]
    unnamed x13 -> x7, other arithmetic: 25.7 us -> 7.1 us
    add x3, other arithmetic: 17.5 us -> 2.87 us  [bypass_terms(): outs_i.append(s_r * imag[k] - s_i * real[k] + cross_r)]
  transfers between devices with their start and end apart: 2 -> 3, of which waited for: 0 -> 2; matrix products, arithmetic and copies ran while one was open for 37% -> 3% of each run, Pallas kernels for 0% -> 21%
where the time goes in v1:
time: 244 us; the launch traced here: 242 us
  waiting for transfers between devices  107 us (44%)
  Pallas kernels  69.5 us (28%)
  blocking collectives  32.2 us (13%)
  other arithmetic  14 us (6%)
  between operations  13.9 us (6%)
  local copies, waits for them, and re-layouts  5.72 us (2%)
    reduce_scatter x2, waiting for transfers between devices, spectrum(): return lax.psum_scatter(parts, 'slab', scatter_dimension=0, tiled=True)[0]  107 us
    pallas_call x2, Pallas kernels, forward_modes(): pl.pallas_call(functools.partial(forward_kernel, plan), grid=(3, planes /...  34.9 us
    pallas_call x1, Pallas kernels, inverse_field(): pl.pallas_call(functools.partial(inverse_kernel, plan, step_planes), grid...  34.6 us
    all_gather x1, blocking collectives, shards(): modes = lax.all_gather(mode_grads, 'slab', axis=0)  32.2 us
    unnamed x7, other arithmetic  7.1 us
  transfers between devices with their start and end apart: 3, of which 2 were waited for; matrix products, arithmetic and copies ran while one was open for 3% of the time, Pallas kernels for 21%

profile of v1, /device:TPU:0, one launch (start us, length us, event | category | flops | bytes accessed | tf_op | source)
XLA Modules:
  0.0 242.3 jit_solution(4518067796344490296)
XLA Ops:
  7.2 0.8 constant_dynamic-slice_fusion
  8.1 1.0 copy-done
  9.1 0.9 copy-done.3
  10.1 17.5 %shard_map.104 = f32[8,3,2,32,128]{4,3,2,1,0:T(8,128)} custom-call(bf16[2,3,32,256,256]{4,3,2,1,0:T(8,128)(2,1)} %bitcast.43, bf16[2,128,256]{2,1,0:T(8,128)(2,1)S(1)} %copy-done.3, bf16[4,256,256]{2,1,0:T(8,128)(2,1)S(1)} %copy-done, bf16[2,64,32]{2,1,0:T(8,128)(2,1)S(1)} %get-tuple-element.9.tab_z), custom_call_target="tpu_custom_call" | custom-call | flops 3221225472 | bytes 25165824 | tf_op jit(solution)/shard_map/pallas_call | solution.py:126
  27.6 17.4 %shard_map.106 = f32[8,3,2,32,128]{4,3,2,1,0:T(8,128)} custom-call(bf16[2,3,32,256,256]{4,3,2,1,0:T(8,128)(2,1)} %bitcast.59, bf16[2,128,256]{2,1,0:T(8,128)(2,1)S(1)} %copy-done.4, bf16[4,256,256]{2,1,0:T(8,128)(2,1)S(1)} %copy-done.1, bf16[2,64,32]{2,1,0:T(8,128)(2,1)S(1)} %get-tuple-element.9.tab_z), custom_call_target="tpu_custom_call" | custom-call | flops 3221225472 | bytes 25165824 | tf_op jit(solution)/shard_map/pallas_call | solution.py:126
  45.4 47.4 %reduce-scatter.3.cloned.1.call-done = f32[1,3,2,32,128]{4,3,2,1,0:T(8,128)} async-done(((f32[8,3,2,32,128]{4,3,2,1,0:T(8,128)}), f32[1,3,2,32,128]{4,3,2,1,0:T(8,128)}) %reduce-scatter.3.cloned.1.call-update) | async-done | bytes 98320 | tf_op jit(solution)/shard_map/reduce_scatter | solution.py:273
  92.9 0.9 subtract_bitcast_fusion
  93.8 1.0 add_bitcast_fusion
  94.8 1.0 subtract_bitcast_fusion.2
  95.7 1.0 add_bitcast_fusion.2
  96.7 1.0 subtract_bitcast_fusion.1
  97.7 1.0 add_bitcast_fusion.1
  98.6 59.3 %reduce-scatter.5.cloned.1.call-done = f32[1,3,2,32,128]{4,3,2,1,0:T(8,128)} async-done(((f32[8,3,2,32,128]{4,3,2,1,0:T(8,128)}), f32[1,3,2,32,128]{4,3,2,1,0:T(8,128)}) %reduce-scatter.5.cloned.1.call-update) | async-done | bytes 98320 | tf_op jit(solution)/shard_map/reduce_scatter | solution.py:273
  158.0 1.1 add_dynamic-update-slice_fusion.4
  159.1 1.0 add_dynamic-update-slice_fusion.3
  160.1 1.0 add_dynamic-update-slice_fusion.2
  161.1 1.0 add_dynamic-update-slice_fusion.1
  162.0 1.1 add_dynamic-update-slice_fusion
  163.1 1.0 subtract_dynamic-update-slice_fusion.2
  164.1 1.0 subtract_dynamic-update-slice_fusion.1
  165.1 1.0 subtract_dynamic-update-slice_fusion
  167.4 32.2 %all-gather = f32[24,2,32,128]{3,2,1,0:T(8,128)S(1)} all-gather(f32[3,2,32,128]{3,2,1,0:T(8,128)S(1)} %pad_maximum_fusion), channel_id=2, replica_groups=mesh['slab'=8,'rep'=4] {'slab'}, dimensions={0}, use_global_device_ids=true | all-gather | bytes 884736 | tf_op jit(solution)/shard_map/all_gather | solution.py:283
  199.6 34.6 %shard_map.105 = bf16[6,32,256,256]{3,2,1,0:T(8,128)(2,1)} custom-call(f32[8]{0:T(128)S(1)} %bitcast.42, bf16[6,32,256,256]{3,2,1,0:T(8,128)(2,1)} %bitcast.44, f32[8,3,2,32,128]{4,3,2,1,0:T(8,128)S(1)} %bitcast.41, bf16[2,32,64]{2,1,0:T(8,128)(2,1)S(1)} %copy.19.tab_z, bf16[384,1024]{1,0:T(8,128)(2,1)S(1)} %copy-done.2, bf16[512,192]{1,0:T(8,128)(2,1)S(1)} %copy-done.5), custom_call_target="tpu_custom_call" | custom-call | flops 4831838208 | bytes 50331648 | tf_op jit(solution)/shard_map/pallas_call | solution.py:232
  234.2 1.6 copy.33
  (29 shorter events, 1.7 us)
Async XLA Ops:
  7.2 85.7 %reduce-scatter.3.cloned.1.call-start = ((), (), s32[]{:S(2)}) async-start(), calls=%async_computation.2 | async-start | bytes 884736 | tf_op jit(solution)/shard_map/reduce_scatter | solution.py:273
  8.1 1.0 copy-start
  9.1 0.9 copy-start.3
  10.0 17.6 %copy-start.1 = (bf16[4,256,256]{2,1,0:T(8,128)(2,1)S(1)}, bf16[4,256,256]{2,1,0:T(8,128)(2,1)}, u32[]{:S(2)}) copy-start(bf16[4,256,256]{2,1,0:T(8,128)(2,1)} %constant.24.clone.tab_y) | copy-start | bytes 1572868
  10.0 17.6 %copy-start.4 = (bf16[2,128,256]{2,1,0:T(8,128)(2,1)S(1)}, bf16[2,128,256]{2,1,0:T(8,128)(2,1)}, u32[]{:S(2)}) copy-start(bf16[2,128,256]{2,1,0:T(8,128)(2,1)} %constant.23.clone.tab_x) | copy-start | bytes 393220
  10.0 35.2 %copy-start.7 = (f32[128,8,1,1,32]{0,4,3,2,1:T(8,128)S(1)}, f32[128,8,1,1,32]{0,4,3,2,1:T(8,128)}, u32[]{:S(2)}) copy-start(f32[128,8,1,1,32]{0,4,3,2,1:T(8,128)} %param.11) | copy-start | bytes 393220
  10.0 189.5 %copy-start.2 = (bf16[384,1024]{1,0:T(8,128)(2,1)S(1)}, bf16[384,1024]{1,0:T(8,128)(2,1)}, u32[]{:S(2)}) copy-start(bf16[384,1024]{1,0:T(8,128)(2,1)} %constant.25.clone.tab_y) | copy-start | bytes 2359300
  10.0 189.5 %copy-start.5 = (bf16[512,192]{1,0:T(8,128)(2,1)S(1)}, bf16[512,192]{1,0:T(8,128)(2,1)}, u32[]{:S(2)}) copy-start(bf16[512,192]{1,0:T(8,128)(2,1)} %constant.26.clone.tab_x) | copy-start | bytes 589828
  10.0 189.5 %copy-start.6 = (f32[8,1,1]{0,2,1:T(1,128)S(1)}, f32[8,1,1]{0,2,1:T(1,128)}, u32[]{:S(2)}) copy-start(f32[8,1,1]{0,2,1:T(1,128)} %param.12) | copy-start | bytes 100
  27.5 130.4 %reduce-scatter.5.cloned.1.call-start = ((), (), s32[]{:S(2)}) async-start(), calls=%async_computation.3 | async-start | bytes 884736 | tf_op jit(solution)/shard_map/reduce_scatter | solution.py:273
  45.1 189.1 %all-reduce.2.cloned.1.call-start = ((), (), s32[]{:S(2)}) async-start(), calls=%async_computation.4 | async-start | bytes 262144 | tf_op jit(solution)/shard_map/psum | solution.py:306
Sparse Core Ops, SparseCore 0:
  27.7 65.1 reduce-scatter.2
  96.5 61.3 reduce-scatter.4
  167.3 30.3 all-reduce.1

commit v2 on v1

--- a/solution.py
+++ b/solution.py
@@ -255,6 +255,149 @@
     )(weight, field, modes, tab_z, jnp.asarray(plan.inv_y), jnp.asarray(plan.inv_x))
 
 
+def weight_terms(inputs_r, inputs_i, grads_r, grads_i):
+    reals = [sum(inputs_r[k] * grads_r[k] + inputs_i[k] * grads_i[k] for k in range(3))]
+    imags = [sum(inputs_r[k] * grads_i[k] - inputs_i[k] * grads_r[k] for k in range(3))]
+    for k in range(3):
+        a, b = (k + 1) % 3, (k + 2) % 3
+        reals.append(
+            inputs_r[a] * grads_i[b] - inputs_r[b] * grads_i[a]
+            - inputs_i[a] * grads_r[b] + inputs_i[b] * grads_r[a]
+        )
+        imags.append(
+            inputs_r[b] * grads_r[a] - inputs_r[a] * grads_r[b]
+            + inputs_i[b] * grads_i[a] - inputs_i[a] * grads_i[b]
+        )
+    return reals, imags
+
+
+def exchange_kernel(
+    lines, grads, inputs, weights, modes, products,
+    from_pair, pair_sum, from_line, mode_own,
+    pair_send, pair_recv, line_send, line_recv, own_send, own_recv, pass_send, pass_recv,
+):
+    me = lax.axis_index("slab")
+    side, place = lax.rem(me, 2), lax.div(me, 2)
+    partner = me + 1 - 2 * side
+    fields = (grads, inputs)
+    half = grads.shape[-1] // 2
+
+    def peer(step):
+        return 2 * lax.rem(place + step, lines) + side
+
+    barrier = pltpu.get_barrier_semaphore()
+    pl.semaphore_signal(
+        barrier, inc=1, device_id={"slab": partner}, device_id_type=pl.DeviceIdType.MESH
+    )
+    for step in range(1, lines):
+        pl.semaphore_signal(
+            barrier, inc=1, device_id={"slab": peer(step)}, device_id_type=pl.DeviceIdType.MESH
+        )
+    pl.semaphore_wait(barrier, lines)
+
+    def send(source, target, send_sem, recv_sem, device):
+        copy = pltpu.make_async_remote_copy(
+            src_ref=source, dst_ref=target, send_sem=send_sem, recv_sem=recv_sem,
+            device_id={"slab": device}, device_id_type=pl.DeviceIdType.MESH,
+        )
+        copy.start()
+        return copy
+
+    started = []
+
+    def to_pair(f):
+        return [
+            send(
+                fields[f].at[:, 1 - side, k], from_pair.at[f, k], pair_send.at[f, k],
+                pair_recv.at[f, k], partner,
+            )
+            for k in range(3)
+        ]
+
+    def to_line(f, copies):
+        sent = []
+        for k in range(3):
+            copies[k].wait_recv()
+            pair_sum[f, k] = fields[f][:, side, k] + from_pair[f, k]
+            sent.append([
+                send(
+                    pair_sum.at[f, k, lax.rem(place + step, lines)], from_line.at[f, k, step - 1],
+                    line_send.at[f, k, step - 1], line_recv.at[f, k, step - 1], peer(step),
+                )
+                for step in range(1, lines)
+            ])
+        return sent
+
+    def collect(f, sent):
+        reals, imags = [], []
+        for k in range(3):
+            total = pair_sum[f, k, place]
+            for step in range(1, lines):
+                sent[k][step - 1].wait_recv()
+                total = total + from_line[f, k, step - 1]
+            reals.append(total[..., :half])
+            imags.append(total[..., half:])
+        return reals, imags
+
+    grads_pair = to_pair(0)
+    grads_line = to_line(0, grads_pair)
+    inputs_pair = to_pair(1)
+    grads_r, grads_i = collect(0, grads_line)
+    mode_r, mode_i = bypass_terms(weights, grads_r, grads_i)
+    for k in range(3):
+        mode_own[k] = jnp.concatenate([mode_r[k], mode_i[k]], axis=-1)
+    own = [
+        send(mode_own, modes.at[me], own_send.at[step - 1], own_recv.at[step - 1], peer(step))
+        for step in range(1, lines)
+    ]
+    passed = [send(mode_own, modes.at[me], pass_send.at[0], pass_recv.at[0], partner)]
+    modes[me] = mode_own[...]
+    inputs_line = to_line(1, inputs_pair)
+    for step in range(1, lines):
+        own[step - 1].wait_recv()
+        block = modes.at[2 * lax.rem(place + lines - step, lines) + side]
+        passed.append(send(block, block, pass_send.at[step], pass_recv.at[step], partner))
+    inputs_r, inputs_i = collect(1, inputs_line)
+    reals, imags = weight_terms(inputs_r, inputs_i, grads_r, grads_i)
+    for term in range(4):
+        products[term] = jnp.concatenate([reals[term], imags[term]], axis=-1)
+    for copy in passed:
+        copy.wait_recv()
+    for copy in grads_pair + inputs_pair + own + passed + sum(grads_line + inputs_line, []):
+        copy.wait_send()
+
+
+def exchange(owners, grads, inputs, weights):
+    lines = owners // 2
+    kept = grads.shape[1:]
+    block = kept[1:]
+    sides = (lines, 2) + kept
+    grads, inputs = grads.reshape(sides), inputs.reshape(sides)
+    vmem = pl.BlockSpec(memory_space=pltpu.VMEM)
+    dma = pltpu.SemaphoreType.DMA
+    return pl.pallas_call(
+        functools.partial(exchange_kernel, lines),
+        in_specs=[vmem, vmem, vmem],
+        out_specs=[vmem, vmem],
+        out_shape=[
+            jax.ShapeDtypeStruct((owners,) + kept, F32),
+            jax.ShapeDtypeStruct((4,) + block, F32),
+        ],
+        scratch_shapes=[
+            pltpu.VMEM((2, 3, lines) + block, F32),
+            pltpu.VMEM((2, 3, lines) + block, F32),
+            pltpu.VMEM((2, 3, lines - 1) + block, F32),
+            pltpu.VMEM(kept, F32),
+            dma((2, 3)), dma((2, 3)),
+            dma((2, 3, lines - 1)), dma((2, 3, lines - 1)),
+            dma((lines - 1,)), dma((lines - 1,)), dma((lines,)), dma((lines,)),
+        ],
+        compiler_params=pltpu.CompilerParams(
+            collective_id=0, has_side_effects=True, vmem_limit_bytes=48 * 2**20
+        ),
+    )(grads, inputs, weights)
+
+
 def shards(saved_input, output_grad, spectral_weight, bypass_weight):
     planes, nx, ny = saved_input.shape[3:]
     rows_owned = spectral_weight.shape[0]
@@ -264,46 +407,27 @@
     depth = lax.dynamic_slice_in_dim(jnp.asarray(plan.fwd_z), start, planes, axis=1)
     tab_fwd = jnp.swapaxes(depth, 1, 2)
 
-    def spectrum(field):
+    def partial_spectrum(field):
         parts = forward_modes(plan, field.reshape(2, 3, planes, nx, ny), tab_fwd)
         if shares > 1:
             parts = parts.reshape(plan.owners, 3, 1, KM, 2, shares, KM // shares)
             parts = jnp.transpose(parts, (0, 5, 1, 2, 3, 4, 6))
             parts = parts.reshape(plan.owners * shares, 3, 1, KM, plan.lanes // shares)
-        return lax.psum_scatter(parts, "slab", scatter_dimension=0, tiled=True)[0]
-
-    grads = spectrum(output_grad)
+        return parts
+
     half = plan.lanes // (2 * shares)
     weights = spectral_weight.reshape(plan.owned_pairs, half, 8, KM)
     weights = jnp.transpose(weights, (2, 0, 3, 1))
-    grads_r = [grads[k, :, :, :half] for k in range(3)]
-    grads_i = [grads[k, :, :, half:] for k in range(3)]
-    mode_r, mode_i = bypass_terms(weights, grads_r, grads_i)
-    mode_grads = jnp.stack([jnp.concatenate([r, i], -1) for r, i in zip(mode_r, mode_i)], 0)
-    modes = lax.all_gather(mode_grads, "slab", axis=0)
+    modes, products = exchange(
+        plan.owners * shares, partial_spectrum(output_grad), partial_spectrum(saved_input), weights
+    )
     if shares > 1:
         modes = modes.reshape(plan.owners, shares, 3, 1, KM, 2, KM // shares)
         modes = jnp.transpose(modes, (0, 2, 3, 4, 5, 1, 6))
         modes = modes.reshape(plan.owners, 3, 1, KM, plan.lanes)
-    inputs = spectrum(saved_input)
-    inputs_r = [inputs[k, :, :, :half] for k in range(3)]
-    inputs_i = [inputs[k, :, :, half:] for k in range(3)]
-    scalar_r = sum(inputs_r[k] * grads_r[k] + inputs_i[k] * grads_i[k] for k in range(3))
-    scalar_i = sum(inputs_r[k] * grads_i[k] - inputs_i[k] * grads_r[k] for k in range(3))
-    vector_r, vector_i = [], []
-    for k in range(3):
-        a, b = (k + 1) % 3, (k + 2) % 3
-        vector_r.append(
-            inputs_r[a] * grads_i[b] - inputs_r[b] * grads_i[a]
-            - inputs_i[a] * grads_r[b] + inputs_i[b] * grads_r[a]
-        )
-        vector_i.append(
-            inputs_r[b] * grads_r[a] - inputs_r[a] * grads_r[b]
-            + inputs_i[b] * grads_i[a] - inputs_i[a] * grads_i[b]
-        )
-    local = jnp.stack([scalar_r] + vector_r + [scalar_i] + vector_i, axis=0)
-    local = jnp.transpose(local, (1, 3, 0, 2)).reshape(rows_owned, 8, 1, 1, KM)
-    weight_grad = lax.psum(local, "rep")
+    weight_grad = lax.psum(products, "rep")
+    weight_grad = weight_grad.reshape(4, plan.owned_pairs, KM, 2, half)
+    weight_grad = jnp.transpose(weight_grad, (1, 4, 3, 0, 2)).reshape(rows_owned, 8, 1, 1, KM)
     input_grad = inverse_field(
         plan, bypass_weight.reshape(8), output_grad.reshape(6, planes, nx, ny), modes, depth
     )

time: 244 us -> 128 us (0.52)
  waiting for transfers between devices: 107 us -> 0.02 us
  Pallas kernels: 69.5 us -> 106 us
  blocking collectives: 32.2 us -> 0 us
  other arithmetic: 14 us -> 0 us
    reduce_scatter x2 -> x0, waiting for transfers between devices: 107 us -> none  [spectrum(): return lax.psum_scatter(parts, 'slab', scatter_dimension=0, tiled=True)[0]]
    pallas_call x0 -> x1, Pallas kernels: none -> 38.1 us  [exchange(): pl.pallas_call(functools.partial(exchange_kernel, lines), in_specs=[vmem,...]
    all_gather x1 -> x0, blocking collectives: 32.2 us -> none  [shards(): modes = lax.all_gather(mode_grads, 'slab', axis=0)]
    unnamed x7 -> x0, other arithmetic: 7.1 us -> none
    sub x3 -> x0, other arithmetic: 2.87 us -> none  [bypass_terms(): outs_r.append(s_r * real[k] + s_i * imag[k] - cross_i)]
    add x3 -> x0, other arithmetic: 2.87 us -> none  [bypass_terms(): outs_i.append(s_r * imag[k] - s_i * real[k] + cross_r)]
  transfers between devices with their start and end apart: 3 -> 1, of which waited for: 2 -> 0; matrix products, arithmetic and copies ran while one was open for 3% -> 0% of each run, Pallas kernels for 21% -> 27%
where the time goes in v2:
time: 128 us; the launch traced here: 127 us
  Pallas kernels  106 us (83%)
  between operations  14.1 us (11%)
  local copies, waits for them, and re-layouts  6.71 us (5%)
    pallas_call x1, Pallas kernels, exchange(): pl.pallas_call(functools.partial(exchange_kernel, lines), in_specs=[vmem,...  38.1 us
    pallas_call x1, Pallas kernels, inverse_field(): pl.pallas_call(functools.partial(inverse_kernel, plan, step_planes), grid...  34.6 us
    pallas_call x2, Pallas kernels, forward_modes(): pl.pallas_call(functools.partial(forward_kernel, plan), grid=(3, planes /...  33.1 us
    unnamed x11, local copies, waits for them, and re-layouts  3.52 us
  transfers between devices with their start and end apart: 1, of which 0 were waited for; matrix products, arithmetic and copies ran while one was open for 0% of the time, Pallas kernels for 27%

profile of v2, /device:TPU:0, one launch (start us, length us, event | category | flops | bytes accessed | tf_op | source)
XLA Modules:
  0.0 126.7 jit_solution(16124186980927942829)
XLA Ops:
  7.2 0.0 all-reduce.2.cloned.1.call-start
  7.2 0.7 constant_dynamic-slice_fusion
  7.9 0.1 copy.15.tab_z
  8.1 1.1 reshape.40
  9.2 0.0 copy-start
  9.2 1.0 copy-done
  10.2 0.0 copy-start.2
  10.2 0.9 copy-done.2
  11.1 0.0 copy-start.1
  11.1 0.0 copy-start.3
  11.1 0.0 copy-start.4
  11.1 16.6 %shard_map.105 = f32[8,3,2,32,128]{4,3,2,1,0:T(8,128)S(1)} custom-call(bf16[2,3,32,256,256]{4,3,2,1,0:T(8,128)(2,1)} %bitcast.29, bf16[2,128,256]{2,1,0:T(8,128)(2,1)S(1)} %copy-done.2, bf16[4,256,256]{2,1,0:T(8,128)(2,1)S(1)} %copy-done, bf16[2,64,32]{2,1,0:T(8,128)(2,1)S(1)} %copy.15.tab_z), custom_call_target="tpu_custom_call" | custom-call | flops 3221225472 | bytes 25165824 | tf_op jit(solution)/shard_map/pallas_call | solution.py:126
  27.8 16.5 %shard_map.104 = f32[8,3,2,32,128]{4,3,2,1,0:T(8,128)S(1)} custom-call(bf16[2,3,32,256,256]{4,3,2,1,0:T(8,128)(2,1)} %bitcast.27, bf16[2,128,256]{2,1,0:T(8,128)(2,1)S(1)} %copy-done.2, bf16[4,256,256]{2,1,0:T(8,128)(2,1)S(1)} %copy-done, bf16[2,64,32]{2,1,0:T(8,128)(2,1)S(1)} %copy.15.tab_z), custom_call_target="tpu_custom_call" | custom-call | flops 3221225472 | bytes 25165824 | tf_op jit(solution)/shard_map/pallas_call | solution.py:126
  44.3 38.1 %shard_map.106 = (f32[8,3,2,32,128]{4,3,2,1,0:T(8,128)S(1)}, f32[4,2,32,128]{3,2,1,0:T(8,128)S(1)}) custom-call(f32[4,2,3,2,32,128]{5,4,3,2,1,0:T(8,128)S(1)} %bitcast.24, f32[4,2,3,2,32,128]{5,4,3,2,1,0:T(8,128)S(1)} %bitcast.23, f32[8,2,32,64]{3,2,1,0:T(8,128)S(1)} %bitcast.25), custom_call_target="tpu_custom_call" | custom-call | tf_op jit(solution)/shard_map/pallas_call | solution.py:378
  82.4 0.2 reshape.42
  82.6 0.2 copy.18
  82.8 0.8 reshape.43
  83.6 0.0 all-reduce.2.cloned.1.call-update
  83.6 0.0 copy-done.1
  83.7 0.0 copy-done.3
  83.7 0.0 copy-done.4
  83.7 34.6 %shard_map.107 = bf16[6,32,256,256]{3,2,1,0:T(8,128)(2,1)} custom-call(f32[8]{0:T(128)S(1)} %bitcast.26, bf16[6,32,256,256]{3,2,1,0:T(8,128)(2,1)} %bitcast.28, f32[8,3,2,32,128]{4,3,2,1,0:T(8,128)S(1)} %get-tuple-element.4.modes, bf16[2,32,64]{2,1,0:T(8,128)(2,1)S(1)} %get-tuple-element.10.tab_z, bf16[384,1024]{1,0:T(8,128)(2,1)S(1)} %copy-done.1, ...), custom_call_target="tpu_custom_call" | custom-call | flops 4831838208 | bytes 50331648 | tf_op jit(solution)/shard_map/pallas_call | solution.py:232
  118.3 0.0 all-reduce.2.cloned.1.call-done
  118.3 1.6 %copy.23 = f32[128,8,1,1,32]{0,4,3,2,1:T(8,128)} copy(f32[128,8,1,1,32]{0,4,3,2,1:T(8,128)} %all-reduce.2.cloned.1.call-done) | data formatting | bytes 262144
  (1 shorter events, 0.0 us)
Async XLA Ops:
  7.2 111.1 %all-reduce.2.cloned.1.call-start = ((), (), s32[]{:S(2)}) async-start(), calls=%async_computation | async-start | bytes 262144 | tf_op jit(solution)/shard_map/psum | solution.py:428
  9.2 1.0 copy-start
  10.2 0.9 copy-start.2
  11.1 72.5 %copy-start.1 = (bf16[384,1024]{1,0:T(8,128)(2,1)S(1)}, bf16[384,1024]{1,0:T(8,128)(2,1)}, u32[]{:S(2)}) copy-start(bf16[384,1024]{1,0:T(8,128)(2,1)} %constant.25.clone.tab_y) | copy-start | bytes 2359300
  11.1 72.5 %copy-start.3 = (bf16[512,192]{1,0:T(8,128)(2,1)S(1)}, bf16[512,192]{1,0:T(8,128)(2,1)}, u32[]{:S(2)}) copy-start(bf16[512,192]{1,0:T(8,128)(2,1)} %constant.26.clone.tab_x) | copy-start | bytes 589828
  11.1 72.5 %copy-start.4 = (f32[8,1,1]{0,2,1:T(1,128)S(1)}, f32[8,1,1]{0,2,1:T(1,128)}, u32[]{:S(2)}) copy-start(f32[8,1,1]{0,2,1:T(1,128)} %param.12) | copy-start | bytes 100
Sparse Core Ops, SparseCore 0:
  83.8 32.3 all-reduce.1

commit v3 on v2

--- a/solution.py
+++ b/solution.py
@@ -89,8 +89,7 @@
         self.fwd_z = np.stack(halves(np.concatenate([cos_z, sin_z], 1)), 0)
 
 
-def forward_kernel(plan, field, tab_x, tab_y, tab_z, out, along_x, along_xy):
-    group = pl.program_id(1)
+def forward_planes(plan, group, field, tab_x, tab_y, along_x, along_xy):
     rows = 2 * KM
     pairs, lanes, zb = plan.pairs, plan.lanes, plan.zb
     for z in range(zb):
@@ -110,14 +109,27 @@
     modes = wide[:, :lanes] + wide[:, lanes:] + narrow
     along_xy[:, pl.ds(pl.multiple_of(group * zb, zb), zb), :] = modes.reshape(pairs, zb, lanes)
 
+
+def forward_depth(plan, tab_z, along_xy, store):
+    for pair in range(plan.pairs):
+        high, low = split(along_xy[pair])
+        turned = dot(tab_z[0], high) + dot(tab_z[1], high) + dot(tab_z[0], low)
+        store(
+            pair // plan.owned_pairs, pair % plan.owned_pairs,
+            turned[:KM] + turn(turned[KM:], -1.0),
+        )
+
+
+def forward_kernel(plan, field, tab_x, tab_y, tab_z, out, along_x, along_xy):
+    group = pl.program_id(1)
+    forward_planes(plan, group, field, tab_x, tab_y, along_x, along_xy)
+
     @pl.when(group == plan.planes // plan.zb - 1)
     def _():
-        for pair in range(pairs):
-            high, low = split(along_xy[pair])
-            turned = dot(tab_z[0], high) + dot(tab_z[1], high) + dot(tab_z[0], low)
-            out[pair // plan.owned_pairs, 0, pair % plan.owned_pairs] = turned[:KM] + turn(
-                turned[KM:], -1.0
-            )
+        def store(owner, pair, values):
+            out[owner, 0, pair] = values
+
+        forward_depth(plan, tab_z, along_xy, store)
 
 
 def forward_modes(plan, field, tab_z):
@@ -367,6 +379,195 @@
         copy.wait_send()
 
 
+def merged_kernel(
+    plan, lines, field, tab_x, tab_y, tab_z, grads, weights, modes_out, products,
+    along_x, along_xy, inputs, modes, spectra,
+    from_pair, pair_sum, from_line, mode_own,
+    pair_send, pair_recv, line_send, line_recv, own_send, own_recv, pass_send, pass_recv,
+):
+    groups = plan.planes // plan.zb
+    group = pl.program_id(1)
+    step_now = pl.program_id(0) * groups + group
+    last = 3 * groups - 1
+    me = lax.axis_index("slab")
+    side, place = lax.rem(me, 2), lax.div(me, 2)
+    partner = me + 1 - 2 * side
+    fields = (grads, inputs)
+    half = plan.lanes // 2
+    line_steps = range(1, lines)
+
+    def peer(step):
+        return 2 * lax.rem(place + step, lines) + side
+
+    def copy(source, target, send_sem, recv_sem, device):
+        return pltpu.make_async_remote_copy(
+            src_ref=source, dst_ref=target, send_sem=send_sem, recv_sem=recv_sem,
+            device_id={"slab": device}, device_id_type=pl.DeviceIdType.MESH,
+        )
+
+    def pair_copy(f, k):
+        return copy(
+            fields[f].at[:, 1 - side, k], from_pair.at[f, k], pair_send.at[f, k],
+            pair_recv.at[f, k], partner,
+        )
+
+    def line_copy(f, k, step):
+        return copy(
+            pair_sum.at[f, k, lax.rem(place + step, lines)], from_line.at[f, k, step - 1],
+            line_send.at[f, k, step - 1], line_recv.at[f, k, step - 1], peer(step),
+        )
+
+    def own_copy(step):
+        return copy(
+            mode_own, modes.at[me], own_send.at[step - 1], own_recv.at[step - 1], peer(step)
+        )
+
+    def pass_copy(step):
+        if step == 0:
+            return copy(mode_own, modes.at[me], pass_send.at[0], pass_recv.at[0], partner)
+        block = modes.at[2 * lax.rem(place + lines - step, lines) + side]
+        return copy(block, block, pass_send.at[step], pass_recv.at[step], partner)
+
+    def to_line(f, k):
+        pair_copy(f, k).wait_recv()
+        pair_sum[f, k] = fields[f][:, side, k] + from_pair[f, k]
+        for step in line_steps:
+            line_copy(f, k, step).start()
+
+    def collect(f):
+        reals, imags = [], []
+        for k in range(3):
+            total = pair_sum[f, k, place]
+            for step in line_steps:
+                line_copy(f, k, step).wait_recv()
+                total = total + from_line[f, k, step - 1]
+            reals.append(total[..., :half])
+            imags.append(total[..., half:])
+        return reals, imags
+
+    def join(real, imag):
+        return jnp.concatenate([real, imag], axis=-1)
+
+    def begin():
+        barrier = pltpu.get_barrier_semaphore()
+        for device in [partner] + [peer(step) for step in line_steps]:
+            pl.semaphore_signal(
+                barrier, inc=1, device_id={"slab": device}, device_id_type=pl.DeviceIdType.MESH
+            )
+        pl.semaphore_wait(barrier, lines)
+        for k in range(3):
+            pair_copy(0, k).start()
+
+    def make_modes():
+        grads_r, grads_i = collect(0)
+        mode_r, mode_i = bypass_terms(weights, grads_r, grads_i)
+        for k in range(3):
+            spectra[k] = join(grads_r[k], grads_i[k])
+            mode_own[k] = join(mode_r[k], mode_i[k])
+        for step in line_steps:
+            own_copy(step).start()
+        pass_copy(0).start()
+        modes[me] = mode_own[...]
+
+    def pass_on():
+        for step in line_steps:
+            own_copy(step).wait_recv()
+            pass_copy(step).start()
+
+    def finish():
+        inputs_r, inputs_i = collect(1)
+        grads_r = [spectra[k, :, :, :half] for k in range(3)]
+        grads_i = [spectra[k, :, :, half:] for k in range(3)]
+        reals, imags = weight_terms(inputs_r, inputs_i, grads_r, grads_i)
+        for term in range(4):
+            products[term] = join(reals[term], imags[term])
+        for step in range(lines):
+            pass_copy(step).wait_recv()
+        modes_out[...] = modes[...]
+        for f in range(2):
+            for k in range(3):
+                pair_copy(f, k).wait_send()
+                for step in line_steps:
+                    line_copy(f, k, step).wait_send()
+        for step in line_steps:
+            own_copy(step).wait_send()
+        for step in range(lines):
+            pass_copy(step).wait_send()
+
+    def at(twelfth, *stages):
+        @pl.when(step_now == min(last, twelfth * groups // 4))
+        def _():
+            for stage in stages:
+                stage()
+
+    at(0, begin)
+    forward_planes(plan, group, field, tab_x, tab_y, along_x, along_xy)
+
+    for k in range(3):
+
+        @pl.when(step_now == (k + 1) * groups - 1)
+        def _(k=k):
+            def store(owner, pair, values):
+                inputs[owner // 2, owner % 2, k, pair] = values
+
+            forward_depth(plan, tab_z, along_xy, store)
+            pair_copy(1, k).start()
+
+    at(2, lambda: to_line(0, 0))
+    at(4, lambda: to_line(0, 1))
+    at(6, lambda: to_line(0, 2))
+    at(8, make_modes, lambda: to_line(1, 0))
+    at(10, pass_on)
+    at(12, lambda: to_line(1, 1), lambda: to_line(1, 2), finish)
+
+
+def merged_exchange(plan, field, tab_z, grads, weights):
+    planes, nx, ny, owners = plan.planes, plan.nx, plan.ny, plan.owners
+    lines = owners // 2
+    kept = grads.shape[1:]
+    block = kept[1:]
+    grads = grads.reshape((lines, 2) + kept)
+    dma = pltpu.SemaphoreType.DMA
+
+    def whole(shape):
+        return pl.BlockSpec(shape, lambda k, g: (0,) * len(shape))
+
+    return pl.pallas_call(
+        functools.partial(merged_kernel, plan, lines),
+        grid=(3, planes // plan.zb),
+        in_specs=[
+            pl.BlockSpec((2, 1, plan.zb, nx, ny), lambda k, g: (0, k, g, 0, 0)),
+            whole(plan.fwd_x.shape),
+            whole(plan.fwd_y.shape),
+            whole((2, 2 * KM, planes)),
+            whole(grads.shape),
+            whole(weights.shape),
+        ],
+        out_specs=[whole((owners,) + kept), whole((4,) + block)],
+        out_shape=[
+            jax.ShapeDtypeStruct((owners,) + kept, F32),
+            jax.ShapeDtypeStruct((4,) + block, F32),
+        ],
+        scratch_shapes=[
+            pltpu.VMEM((ny // 128, 2 * KM * plan.zb, 128), F32),
+            pltpu.VMEM((plan.pairs, planes, plan.lanes), F32),
+            pltpu.VMEM(grads.shape, F32),
+            pltpu.VMEM((owners,) + kept, F32),
+            pltpu.VMEM(kept, F32),
+            pltpu.VMEM((2, 3, lines) + block, F32),
+            pltpu.VMEM((2, 3, lines) + block, F32),
+            pltpu.VMEM((2, 3, lines - 1) + block, F32),
+            pltpu.VMEM(kept, F32),
+            dma((2, 3)), dma((2, 3)),
+            dma((2, 3, lines - 1)), dma((2, 3, lines - 1)),
+            dma((lines - 1,)), dma((lines - 1,)), dma((lines,)), dma((lines,)),
+        ],
+        compiler_params=pltpu.CompilerParams(
+            collective_id=1, has_side_effects=True, vmem_limit_bytes=48 * 2**20
+        ),
+    )(field, jnp.asarray(plan.fwd_x), jnp.asarray(plan.fwd_y), tab_z, grads, weights)
+
+
 def exchange(owners, grads, inputs, weights):
     lines = owners // 2
     kept = grads.shape[1:]
@@ -418,10 +619,13 @@
     half = plan.lanes // (2 * shares)
     weights = spectral_weight.reshape(plan.owned_pairs, half, 8, KM)
     weights = jnp.transpose(weights, (2, 0, 3, 1))
-    modes, products = exchange(
-        plan.owners * shares, partial_spectrum(output_grad), partial_spectrum(saved_input), weights
-    )
-    if shares > 1:
+    grads = partial_spectrum(output_grad)
+    if shares == 1:
+        field = saved_input.reshape(2, 3, planes, nx, ny)
+        modes, products = merged_exchange(plan, field, tab_fwd, grads, weights)
+    else:
+        inputs = partial_spectrum(saved_input)
+        modes, products = exchange(plan.owners * shares, grads, inputs, weights)
         modes = modes.reshape(plan.owners, shares, 3, 1, KM, 2, KM // shares)
         modes = jnp.transpose(modes, (0, 2, 3, 4, 5, 1, 6))
         modes = modes.reshape(plan.owners, 3, 1, KM, plan.lanes)

time: 128 us -> 118 us (0.922)
  Pallas kernels: 106 us -> 96.1 us
    pallas_call x2 -> x1, Pallas kernels: 33.1 us -> 16.6 us  [forward_modes(): pl.pallas_call(functools.partial(forward_kernel, plan), grid=(3, planes /...]
    pallas_call x1, Pallas kernels: 38.1 us -> 44.9 us  [merged_exchange(): pl.pallas_call(functools.partial(merged_kernel, plan, lines), grid=(3, pl...]
    unnamed x11 -> x15, local copies, waits for them, and re-layouts: 3.52 us -> 3.53 us
  transfers between devices with their start and end apart: 1 -> 1, of which waited for: 0 -> 0; matrix products, arithmetic and copies ran while one was open for 0% -> 0% of each run, Pallas kernels for 27% -> 30%
where the time goes in v3:
time: 118 us; the launch traced here: 117 us
  Pallas kernels  96.1 us (81%)
  between operations  14.1 us (12%)
  local copies, waits for them, and re-layouts  6.77 us (6%)
    pallas_call x1, Pallas kernels, merged_exchange(): pl.pallas_call(functools.partial(merged_kernel, plan, lines), grid=(3, pl...  44.9 us
    pallas_call x1, Pallas kernels, inverse_field(): pl.pallas_call(functools.partial(inverse_kernel, plan, step_planes), grid...  34.6 us
    pallas_call x1, Pallas kernels, forward_modes(): pl.pallas_call(functools.partial(forward_kernel, plan), grid=(3, planes /...  16.6 us
    unnamed x15, local copies, waits for them, and re-layouts  3.53 us
  transfers between devices with their start and end apart: 1, of which 0 were waited for; matrix products, arithmetic and copies ran while one was open for 0% of the time, Pallas kernels for 30%

profile of v3, /device:TPU:0, one launch (start us, length us, event | category | flops | bytes accessed | tf_op | source)
XLA Modules:
  0.0 117.1 jit_solution(6861873306851232108)
XLA Ops:
  7.2 0.0 copy-start.1
  7.2 0.0 copy-start.4
  7.2 0.0 all-reduce.2.cloned.1.call-start
  7.2 0.8 constant_dynamic-slice_fusion
  8.0 0.1 copy.17.tab_z
  8.1 1.1 reshape.36
  9.3 0.0 copy-start
  9.3 1.0 copy-done
  10.3 0.0 copy-start.3
  10.3 0.9 copy-done.3
  11.2 0.0 copy-start.2
  11.2 16.6 %shard_map.104 = f32[8,3,2,32,128]{4,3,2,1,0:T(8,128)S(1)} custom-call(bf16[2,3,32,256,256]{4,3,2,1,0:T(8,128)(2,1)} %bitcast.25, bf16[2,128,256]{2,1,0:T(8,128)(2,1)S(1)} %copy-done.3, bf16[4,256,256]{2,1,0:T(8,128)(2,1)S(1)} %copy-done, bf16[2,64,32]{2,1,0:T(8,128)(2,1)S(1)} %copy.17.tab_z), custom_call_target="tpu_custom_call" | custom-call | flops 3221225472 | bytes 25165824 | tf_op jit(solution)/shard_map/pallas_call | solution.py:138
  27.8 0.0 copy-done.1
  27.8 0.0 copy-done.4
  27.9 44.9 %shard_map.105 = (f32[8,3,2,32,128]{4,3,2,1,0:T(8,128)S(1)}, f32[4,2,32,128]{3,2,1,0:T(8,128)S(1)}) custom-call(bf16[2,3,32,256,256]{4,3,2,1,0:T(8,128)(2,1)} %bitcast.27, bf16[2,128,256]{2,1,0:T(8,128)(2,1)S(1)} %copy-done.4, bf16[4,256,256]{2,1,0:T(8,128)(2,1)S(1)} %copy-done.1, bf16[2,64,32]{2,1,0:T(8,128)(2,1)S(1)} %copy.17.tab_z, ...), custom_call_target="tpu_custom_call" | custom-call | tf_op jit(solution)/shard_map/pallas_call | solution.py:535
  72.8 0.2 reshape.38
  73.0 0.2 copy.18
  73.2 0.8 reshape.39
  74.0 0.0 all-reduce.2.cloned.1.call-update
  74.1 0.0 copy-done.2
  74.1 0.0 copy-done.5
  74.1 0.0 copy-done.6
  74.1 34.6 %shard_map.106 = bf16[6,32,256,256]{3,2,1,0:T(8,128)(2,1)} custom-call(f32[8]{0:T(128)S(1)} %bitcast.24, bf16[6,32,256,256]{3,2,1,0:T(8,128)(2,1)} %bitcast.26, f32[8,3,2,32,128]{4,3,2,1,0:T(8,128)S(1)} %get-tuple-element.4.modes, bf16[2,32,64]{2,1,0:T(8,128)(2,1)S(1)} %get-tuple-element.10.tab_z, bf16[384,1024]{1,0:T(8,128)(2,1)S(1)} %copy-done.2, ...), custom_call_target="tpu_custom_call" | custom-call | flops 4831838208 | bytes 50331648 | tf_op jit(solution)/shard_map/pallas_call | solution.py:244
  108.7 1.6 %copy.23 = f32[128,8,1,1,32]{0,4,3,2,1:T(8,128)} copy(f32[128,8,1,1,32]{0,4,3,2,1:T(8,128)} %all-reduce.2.cloned.1.call-done) | data formatting | bytes 262144
  (4 shorter events, 0.0 us)
Async XLA Ops:
  7.2 20.7 %copy-start.1 = (bf16[4,256,256]{2,1,0:T(8,128)(2,1)S(1)}, bf16[4,256,256]{2,1,0:T(8,128)(2,1)}, u32[]{:S(2)}) copy-start(bf16[4,256,256]{2,1,0:T(8,128)(2,1)} %constant.24.clone.tab_y) | copy-start | bytes 1572868
  7.2 20.7 %copy-start.4 = (bf16[2,128,256]{2,1,0:T(8,128)(2,1)S(1)}, bf16[2,128,256]{2,1,0:T(8,128)(2,1)}, u32[]{:S(2)}) copy-start(bf16[2,128,256]{2,1,0:T(8,128)(2,1)} %constant.23.clone.tab_x) | copy-start | bytes 393220
  7.2 101.5 %all-reduce.2.cloned.1.call-start = ((), (), s32[]{:S(2)}) async-start(), calls=%async_computation | async-start | bytes 262144 | tf_op jit(solution)/shard_map/psum | solution.py:632
  9.3 1.0 copy-start
  10.3 0.9 copy-start.3
  11.2 62.8 %copy-start.2 = (bf16[384,1024]{1,0:T(8,128)(2,1)S(1)}, bf16[384,1024]{1,0:T(8,128)(2,1)}, u32[]{:S(2)}) copy-start(bf16[384,1024]{1,0:T(8,128)(2,1)} %constant.25.clone.tab_y) | copy-start | bytes 2359300
  11.2 62.9 %copy-start.5 = (bf16[512,192]{1,0:T(8,128)(2,1)S(1)}, bf16[512,192]{1,0:T(8,128)(2,1)}, u32[]{:S(2)}) copy-start(bf16[512,192]{1,0:T(8,128)(2,1)} %constant.26.clone.tab_x) | copy-start | bytes 589828
  11.2 62.9 %copy-start.6 = (f32[8,1,1]{0,2,1:T(1,128)S(1)}, f32[8,1,1]{0,2,1:T(1,128)}, u32[]{:S(2)}) copy-start(f32[8,1,1]{0,2,1:T(1,128)} %param.12) | copy-start | bytes 100
Sparse Core Ops, SparseCore 0:
  74.2 30.8 all-reduce.1
